TPU v7x, 768 devices: a whole 4x8x12 slice. The times are simulated.
768 devices in a mesh: grp: 12 (over z), loc: 64 (over x, y, core).
Axes of the slice: x: 4, y: 8, z: 12, core: 2. Of those that a mesh axis runs over, the one named last changes fastest.
Arguments:
- tokens: bfloat16 [1536, 7168], P('grp', 'loc'), may hold values from -6 to 6
- expert_ids: int32 [1536, 8], P('grp'), may hold values from 0 to 191, as said below
- gate_weights: float32 [1536, 8], P('grp'), may hold values from 0.05 to 1
- gate_blocks: bfloat16 [768, 1792, 256], P(('grp', 'loc')), may hold values from -0.0625 to 0.0625
- up_blocks: bfloat16 [768, 1792, 256], P(('grp', 'loc')), may hold values from -0.0625 to 0.0625
- down_blocks: bfloat16 [768, 256, 1792], P(('grp', 'loc')), may hold values from -0.125 to 0.125
Outputs:
- combined: bfloat16 [1536, 7168], P('grp', 'loc')
Inputs may be any that keep to these rules, and one draw needn't show every extreme that they name: `expert_ids`: each row names 8 different experts, all lying in at most 4 groups, where expert e lies in group e // 16.
All inputs are finite; a program needn't handle non-finite values.
Results may differ from a plain program's by a relative error of at most 0.0058.
Values may be sent and summed in bfloat16 or wider, within the bound.
A program may use at most 32 MiB of HBM per device.

v0:
```python
import jax
import jax.numpy as jnp
from jax import lax
from jax.sharding import PartitionSpec as P

D = 7168
FF = 2048
GRP_EXP = 16


def from_partner(x, axis, distance):
    return lax.ppermute(x, axis, [(i, i ^ 1 << distance) for i in range(lax.axis_size(axis))])


def bin_layout(expert_ids, group_count, capacity, window_experts):
    expert_total = group_count * GRP_EXP
    expert_range = jnp.arange(expert_total, dtype=jnp.int32)[None, :]
    onehot_hits = jnp.zeros((expert_ids.shape[0], expert_total), jnp.int32)
    for column_index in range(expert_ids.shape[1]):
        onehot_hits = onehot_hits + (
            expert_ids[:, column_index : column_index + 1] == expert_range
        ).astype(jnp.int32)
    earlier = jnp.cumsum(onehot_hits, axis=0) - onehot_hits
    slot_index = jnp.take_along_axis(earlier, expert_ids, axis=1)
    within = expert_ids % GRP_EXP
    target = expert_ids // GRP_EXP
    usable = (within < window_experts) & (slot_index < capacity)
    position = (
        target * capacity + jnp.minimum(slot_index, capacity - 1)
    ) * window_experts + jnp.minimum(within, window_experts - 1)
    return (usable, position)


def shards(tokens, expert_ids, gate_weights, gate_blocks, up_blocks, down_blocks):
    group_count = lax.axis_size("grp")
    local_count = lax.axis_size("loc")
    local_index = lax.axis_index("loc")
    token_rows, features = tokens.shape
    choose_count = expert_ids.shape[1]
    block_rows = gate_blocks.shape[1]
    hidden_units = gate_blocks.shape[2]
    depth_split = D // block_rows
    hidden_split = FF // hidden_units
    window_experts = local_count // (depth_split * hidden_split)
    narrow = features // depth_split
    capacity = 8 * (9 * token_rows * choose_count // (32 * group_count * GRP_EXP))
    part_rows = capacity // hidden_split
    low_bits = hidden_split.bit_length() - 1
    usable, position = bin_layout(expert_ids, group_count, capacity, window_experts)
    bin_total = group_count * capacity * window_experts
    bin_range = jnp.arange(bin_total, dtype=jnp.int32)[:, None]
    selector = jnp.zeros((bin_total, token_rows), jnp.bool_)
    for column_index in range(choose_count):
        selector = (
            selector
            | (position[:, column_index][None, :] == bin_range) & usable[:, column_index][None, :]
        )
    outgoing = jnp.dot(
        selector.astype(jnp.bfloat16), tokens, preferred_element_type=jnp.float32
    ).astype(jnp.bfloat16)
    outgoing = outgoing.reshape(group_count, capacity, window_experts, features)
    arrived = lax.all_to_all(outgoing, "grp", split_axis=0, concat_axis=0, tiled=True)
    widened = jnp.broadcast_to(
        arrived.reshape(group_count, capacity, window_experts, depth_split, 1, narrow),
        (group_count, capacity, window_experts, depth_split, hidden_split, narrow),
    )
    widened = widened.reshape(group_count, capacity, local_count * narrow)
    received = lax.all_to_all(widened, "loc", split_axis=2, concat_axis=2, tiled=True)
    received = received.reshape(group_count, hidden_split, part_rows, block_rows)
    gate_pre = jnp.einsum(
        "shrd,dk->hsrk", received, gate_blocks[0], preferred_element_type=jnp.float32
    )
    up_pre = jnp.einsum("shrd,dk->hsrk", received, up_blocks[0], preferred_element_type=jnp.float32)
    summed = jnp.stack([gate_pre, up_pre])
    for bit_index in range(low_bits, low_bits + depth_split.bit_length() - 1):
        summed = summed + from_partner(summed, "loc", bit_index)
    hidden = (jax.nn.silu(summed[0]) * summed[1]).astype(jnp.bfloat16)
    partial_value = jnp.dot(
        hidden.reshape(-1, hidden_units), down_blocks[0], preferred_element_type=jnp.float32
    )
    current = partial_value.reshape(hidden_split, group_count, part_rows, block_rows)
    for bit_index in reversed(range(low_bits)):
        half_rows = current.shape[0] // 2
        upper_half = local_index >> bit_index & 1 == 1
        kept_rows = jnp.where(upper_half, current[half_rows:], current[:half_rows])
        given_rows = jnp.where(upper_half, current[:half_rows], current[half_rows:])
        current = kept_rows + from_partner(given_rows, "loc", bit_index)
    finished = current[0].astype(jnp.bfloat16).reshape(group_count, part_rows, local_count, narrow)
    homeward = lax.all_to_all(
        lax.all_to_all(finished, "grp", split_axis=0, concat_axis=0, tiled=True),
        "loc",
        split_axis=2,
        concat_axis=2,
        tiled=True,
    )
    arranged = homeward.reshape(
        group_count, part_rows, window_experts, depth_split, hidden_split, narrow
    )
    back_flat = arranged.transpose(0, 4, 1, 2, 3, 5).reshape(bin_total, features)
    weights = jnp.where(usable, gate_weights, jnp.zeros_like(gate_weights))
    combined = jnp.zeros((token_rows, features), jnp.float32)
    for column_index in range(choose_count):
        picked_rows = jnp.take(back_flat, position[:, column_index], axis=0).astype(jnp.float32)
        combined = combined + weights[:, column_index : column_index + 1] * picked_rows
    return combined.astype(jnp.bfloat16)


def solution(mesh):
    in_specs = (
        P("grp", "loc"),
        P("grp", None),
        P("grp", None),
        P(("grp", "loc"), None, None),
        P(("grp", "loc"), None, None),
        P(("grp", "loc"), None, None),
    )
    out_specs = P("grp", "loc")
    return jax.shard_map(shards, mesh=mesh, in_specs=in_specs, out_specs=out_specs, check_vma=False)
```

profile of v0, /device:TPU:1, one launch (start us, length us, event | category | flops | bytes accessed | tf_op | source)
XLA Modules:
  0.0 184.0 jit_solution(328791166183138305)
XLA Ops:
  0.0 1.0 slice_bitcast_fusion.31
  1.0 0.7 bitcast_or_fusion
  1.7 0.2 convert_add_fusion
  1.9 0.2 reduce_window_sum.11
  2.1 0.2 fusion.46
  2.5 8.6 %gather_fusion = s32[1024]{0:T(1024)S(1)} fusion(s32[128,192]{1,0:T(8,128)S(1)} %fusion.46, s32[1024]{0:T(1024)S(1)} %reshape.200), kind=kCustom, calls=%fused_computation.8 | custom fusion | bytes 16384 | tf_op jit(solution)/shard_map/jit(take_along_axis)/gather | solution.py:24
  11.4 0.2 convolution_convert_fusion
  11.6 25.2 %all_to_all.20 = bf16[12,8,2,112]{3,2,1,0:T(2,128)(2,1)S(1)} all-to-all(bf16[12,8,2,112]{3,2,1,0:T(2,128)(2,1)S(1)} %bitcast.149), channel_id=1, replica_groups=mesh['grp'=12,'loc'=64] {'grp'}, dimensions={0} | all-to-all | bytes 86016 | tf_op jit(solution)/shard_map/all_to_all | solution.py:62
  36.8 0.3 copy.75
  37.1 2.3 %broadcast_in_dim.28 = bf16[12,8,2,4,8,28]{0,1,5,4,3,2:T(8,128)(2,1)} broadcast(bf16[12,8,2,4,28]{0,1,4,3,2:T(8,128)(2,1)S(1)} %bitcast.143), dimensions={0,1,2,3,5} | broadcast | bytes 387072 | tf_op jit(solution)/shard_map/broadcast_in_dim | solution.py:63
  39.5 5.7 %reshape.237 = bf16[64,2,1344]{2,1,0:T(2,128)(2,1)S(1)} reshape(bf16[1792,8,12]{2,1,0:T(8,128)(2,1)} %bitcast.141) | data formatting | bytes 688128
  45.1 26.0 %all_to_all.21 = bf16[64,2,1344]{2,1,0:T(2,128)(2,1)S(1)} all-to-all(bf16[64,2,1344]{2,1,0:T(2,128)(2,1)S(1)} %reshape.237), channel_id=1, replica_groups=mesh['grp'=12,'loc'=64] {'loc'}, dimensions={0} | all-to-all | bytes 688128 | tf_op jit(solution)/shard_map/all_to_all | solution.py:68
  71.2 6.1 %reshape.238 = bf16[1792,8,12]{2,1,0:T(8,128)(2,1)} reshape(bf16[64,2,1344]{2,1,0:T(2,128)(2,1)S(1)} %all_to_all.21) | data formatting | bytes 688128
  77.3 4.6 %copy.67 = bf16[12,8,1792]{2,1,0:T(8,128)(2,1)S(1)} copy(bf16[12,8,1792]{0,1,2:T(8,128)(2,1)} %bitcast.142) | data formatting | bytes 688128 | tf_op jit(solution)/shard_map/all_to_all | solution.py:68
  81.9 0.3 convolution_bitcast_fusion
  82.2 0.3 convolution_bitcast_fusion.1
  82.5 4.4 %collective-permute-start = (f32[2,8,12,1,256]{4,1,2,3,0:T(8,128)S(1)}, f32[2,8,12,1,256]{4,1,2,3,0:T(8,128)S(1)}, u32[]{:S(2)}, u32[]{:S(2)}) collective-permute-start(f32[2,8,12,1,256]{4,1,2,3,0:T(8,128)S(1)} %pad_maximum_fusion), channel_id=1, source_target_pairs={{0,8},{1,9},{2,10},{3,11},{4,12},{5,13},{6,14},{7,15},{8,0},{9,1},... | collective-permute-start | bytes 589832 | tf_op jit(solution)/shard_map/ppermute | solution.py:12
  86.9 9.6 %collective-permute-done = f32[2,8,12,1,256]{4,1,2,3,0:T(8,128)S(1)} collective-permute-done((f32[2,8,12,1,256]{4,1,2,3,0:T(8,128)S(1)}, f32[2,8,12,1,256]{4,1,2,3,0:T(8,128)S(1)}, u32[]{:S(2)}, u32[]{:S(2)}) %collective-permute-start) | collective-permute-done | bytes 196640 | tf_op jit(solution)/shard_map/ppermute | solution.py:12
  96.6 3.0 %collective-permute-start.1 = (f32[2,8,12,1,256]{4,1,2,3,0:T(8,128)S(1)}, f32[2,8,12,1,256]{4,1,2,3,0:T(8,128)S(1)}, u32[]{:S(2)}, u32[]{:S(2)}) collective-permute-start(f32[2,8,12,1,256]{4,1,2,3,0:T(8,128)S(1)} %fusion.47), channel_id=1, source_target_pairs={{0,16},{1,17},{2,18},{3,19},{4,20},{5,21},{6,22},{7,23},{8,24},{9,... | collective-permute-start | bytes 589832 | tf_op jit(solution)/shard_map/ppermute | solution.py:12
  99.6 3.9 %collective-permute-done.1 = f32[2,8,12,1,256]{4,1,2,3,0:T(8,128)S(1)} collective-permute-done((f32[2,8,12,1,256]{4,1,2,3,0:T(8,128)S(1)}, f32[2,8,12,1,256]{4,1,2,3,0:T(8,128)S(1)}, u32[]{:S(2)}, u32[]{:S(2)}) %collective-permute-start.1) | collective-permute-done | bytes 196640 | tf_op jit(solution)/shard_map/ppermute | solution.py:12
  103.6 0.3 fusion
  104.0 5.4 %collective-permute-start.2 = (f32[4,12,1,1792]{3,1,0,2:T(8,128)S(1)}, f32[4,12,1,1792]{3,1,0,2:T(8,128)S(1)}, u32[]{:S(2)}, u32[]{:S(2)}) collective-permute-start(f32[4,12,1,1792]{3,1,0,2:T(8,128)S(1)} %select_n.100), channel_id=1, source_target_pairs={{0,4},{1,5},{2,6},{3,7},{4,0},{5,1},{6,2},{7,3},{8,12},{9,13},{10,... | collective-permute-start | bytes 1032200 | tf_op jit(solution)/shard_map/ppermute | solution.py:12
  109.5 20.5 %collective-permute-done.2 = f32[4,12,1,1792]{3,1,0,2:T(8,128)S(1)} collective-permute-done((f32[4,12,1,1792]{3,1,0,2:T(8,128)S(1)}, f32[4,12,1,1792]{3,1,0,2:T(8,128)S(1)}, u32[]{:S(2)}, u32[]{:S(2)}) %collective-permute-start.2) | collective-permute-done | bytes 344096 | tf_op jit(solution)/shard_map/ppermute | solution.py:12
  130.1 1.9 %collective-permute-start.3 = (f32[2,12,1,1792]{3,1,0,2:T(8,128)S(1)}, f32[2,12,1,1792]{3,1,0,2:T(8,128)S(1)}, u32[]{:S(2)}, u32[]{:S(2)}) collective-permute-start(f32[2,12,1,1792]{3,1,0,2:T(8,128)S(1)} %slice_select_fusion.2), channel_id=1, source_target_pairs={{0,2},{1,3},{2,0},{3,1},{4,6},{5,7},{6,4},{7,5},{8,10},{9,11},{10,... | collective-permute-start | bytes 516104 | tf_op jit(solution)/shard_map/ppermute | solution.py:12
  132.0 6.4 %collective-permute-done.3 = f32[2,12,1,1792]{3,1,0,2:T(8,128)S(1)} collective-permute-done((f32[2,12,1,1792]{3,1,0,2:T(8,128)S(1)}, f32[2,12,1,1792]{3,1,0,2:T(8,128)S(1)}, u32[]{:S(2)}, u32[]{:S(2)}) %collective-permute-start.3) | collective-permute-done | bytes 172064 | tf_op jit(solution)/shard_map/ppermute | solution.py:12
  138.5 3.5 %collective-permute-start.4 = (f32[1,12,1,1792]{3,1,0,2:T(8,128)S(1)}, f32[1,12,1,1792]{3,1,0,2:T(8,128)S(1)}, u32[]{:S(2)}, u32[]{:S(2)}) collective-permute-start(f32[1,12,1,1792]{3,1,0,2:T(8,128)S(1)} %slice_select_fusion.3), channel_id=1, source_target_pairs={{0,1},{1,0},{2,3},{3,2},{4,5},{5,4},{6,7},{7,6},{8,9},{9,8},{10,11... | collective-permute-start | bytes 258056 | tf_op jit(solution)/shard_map/ppermute | solution.py:12
  142.0 0.9 collective-permute-done.4
  143.0 0.5 convert_element_type.91
  143.5 0.2 copy.70
  143.6 0.7 reshape.239
  144.4 3.5 %all-to-all-start.2 = ((bf16[12,2,896]{2,1,0:T(2,128)(2,1)}), bf16[12,2,896]{2,1,0:T(2,128)(2,1)S(1)}, u32[]{:S(2)}, u32[]{:S(2)}) async-start(bf16[12,2,896]{2,1,0:T(2,128)(2,1)} %reshape.239), calls=%async_computation.2 | async-start | bytes 86016 | tf_op jit(solution)/shard_map/all_to_all | solution.py:90
  147.9 9.3 %all-to-all-done.2 = bf16[12,2,896]{2,1,0:T(2,128)(2,1)S(1)} async-done(((bf16[12,2,896]{2,1,0:T(2,128)(2,1)}), bf16[12,2,896]{2,1,0:T(2,128)(2,1)S(1)}, u32[]{:S(2)}, u32[]{:S(2)}) %all-to-all-start.2) | async-done | bytes 43040 | tf_op jit(solution)/shard_map/all_to_all | solution.py:90
  157.3 0.3 copy.71
  157.6 0.9 reshape.241
  158.5 8.4 %all-to-all-start.3 = ((bf16[64,2,168]{2,1,0:T(2,128)(2,1)}), bf16[64,2,168]{2,1,0:T(2,128)(2,1)S(1)}, u32[]{:S(2)}, u32[]{:S(2)}) async-start(bf16[64,2,168]{2,1,0:T(2,128)(2,1)} %reshape.241), calls=%async_computation.3 | async-start | bytes 131072 | tf_op jit(solution)/shard_map/all_to_all | solution.py:89
  167.0 9.8 %all-to-all-done.3 = bf16[64,2,168]{2,1,0:T(2,128)(2,1)S(1)} async-done(((bf16[64,2,168]{2,1,0:T(2,128)(2,1)}), bf16[64,2,168]{2,1,0:T(2,128)(2,1)S(1)}, u32[]{:S(2)}, u32[]{:S(2)}) %all-to-all-start.3) | async-done | bytes 43040 | tf_op jit(solution)/shard_map/all_to_all | solution.py:89
  176.7 0.2 reshape.242
  177.1 0.1 reshape.135
  177.2 0.7 gather_fusion.1
  177.9 0.7 gather_fusion.2
  178.7 0.7 gather_fusion.3
  179.4 0.7 gather_fusion.4
  180.1 0.7 gather_fusion.5
  180.8 0.7 gather_fusion.6
  181.5 0.7 gather_fusion.7
  182.2 0.7 gather_fusion.8
  182.9 0.3 add_convert_fusion.1
  183.3 0.7 copy.74
  (43 shorter events, 1.1 us)
Async XLA Ops:
  0.0 103.6 %copy-start = (bf16[1,256,1792]{2,1,0:T(8,128)(2,1)S(1)}, bf16[1,256,1792]{2,1,0:T(8,128)(2,1)}, u32[]{:S(2)}) copy-start(bf16[1,256,1792]{2,1,0:T(8,128)(2,1)} %param.13) | copy-start | bytes 2752516
  2.5 8.8 %copy-start.3 = (s32[128,8]{0,1:T(8,128)S(1)}, s32[128,8]{0,1:T(8,128)}, u32[]{:S(2)}) copy-start(s32[128,8]{0,1:T(8,128)} %param.9) | copy-start | bytes 12292
  2.5 8.8 %copy-start.4 = (f32[128,8]{0,1:T(8,128)S(1)}, f32[128,8]{0,1:T(8,128)}, u32[]{:S(2)}) copy-start(f32[128,8]{0,1:T(8,128)} %param.10) | copy-start | bytes 12292
  2.5 8.9 %copy-start.5 = (bf16[128,112]{0,1:T(8,128)(2,1)S(1)}, bf16[128,112]{0,1:T(8,128)(2,1)}, u32[]{:S(2)}) copy-start(bf16[128,112]{0,1:T(8,128)(2,1)} %param.8) | copy-start | bytes 86020
  71.2 10.7 %copy-start.1 = (bf16[1,1792,256]{2,1,0:T(8,128)(2,1)S(1)}, bf16[1,1792,256]{2,1,0:T(8,128)(2,1)}, u32[]{:S(2)}) copy-start(bf16[1,1792,256]{2,1,0:T(8,128)(2,1)} %param.12) | copy-start | bytes 2752516
  77.3 4.9 %copy-start.2 = (bf16[1,1792,256]{2,1,0:T(8,128)(2,1)S(1)}, bf16[1,1792,256]{2,1,0:T(8,128)(2,1)}, u32[]{:S(2)}) copy-start(bf16[1,1792,256]{2,1,0:T(8,128)(2,1)} %param.11) | copy-start | bytes 2752516
  82.5 14.1 %collective-permute-start = (f32[2,8,12,1,256]{4,1,2,3,0:T(8,128)S(1)}, f32[2,8,12,1,256]{4,1,2,3,0:T(8,128)S(1)}, u32[]{:S(2)}, u32[]{:S(2)}) collective-permute-start(f32[2,8,12,1,256]{4,1,2,3,0:T(8,128)S(1)} %pad_maximum_fusion), channel_id=1, source_target_pairs={{0,8},{1,9},{2,10},{3,11},{4,12},{5,13},{6,14},{7,15},{8,0},{9,1},... | collective-permute-start | bytes 589832 | tf_op jit(solution)/shard_map/ppermute | solution.py:12
  96.6 6.9 %collective-permute-start.1 = (f32[2,8,12,1,256]{4,1,2,3,0:T(8,128)S(1)}, f32[2,8,12,1,256]{4,1,2,3,0:T(8,128)S(1)}, u32[]{:S(2)}, u32[]{:S(2)}) collective-permute-start(f32[2,8,12,1,256]{4,1,2,3,0:T(8,128)S(1)} %fusion.47), channel_id=1, source_target_pairs={{0,16},{1,17},{2,18},{3,19},{4,20},{5,21},{6,22},{7,23},{8,24},{9,... | collective-permute-start | bytes 589832 | tf_op jit(solution)/shard_map/ppermute | solution.py:12
  104.0 26.0 %collective-permute-start.2 = (f32[4,12,1,1792]{3,1,0,2:T(8,128)S(1)}, f32[4,12,1,1792]{3,1,0,2:T(8,128)S(1)}, u32[]{:S(2)}, u32[]{:S(2)}) collective-permute-start(f32[4,12,1,1792]{3,1,0,2:T(8,128)S(1)} %select_n.100), channel_id=1, source_target_pairs={{0,4},{1,5},{2,6},{3,7},{4,0},{5,1},{6,2},{7,3},{8,12},{9,13},{10,... | collective-permute-start | bytes 1032200 | tf_op jit(solution)/shard_map/ppermute | solution.py:12
  130.1 8.4 %collective-permute-start.3 = (f32[2,12,1,1792]{3,1,0,2:T(8,128)S(1)}, f32[2,12,1,1792]{3,1,0,2:T(8,128)S(1)}, u32[]{:S(2)}, u32[]{:S(2)}) collective-permute-start(f32[2,12,1,1792]{3,1,0,2:T(8,128)S(1)} %slice_select_fusion.2), channel_id=1, source_target_pairs={{0,2},{1,3},{2,0},{3,1},{4,6},{5,7},{6,4},{7,5},{8,10},{9,11},{10,... | collective-permute-start | bytes 516104 | tf_op jit(solution)/shard_map/ppermute | solution.py:12
  138.5 4.4 %collective-permute-start.4 = (f32[1,12,1,1792]{3,1,0,2:T(8,128)S(1)}, f32[1,12,1,1792]{3,1,0,2:T(8,128)S(1)}, u32[]{:S(2)}, u32[]{:S(2)}) collective-permute-start(f32[1,12,1,1792]{3,1,0,2:T(8,128)S(1)} %slice_select_fusion.3), channel_id=1, source_target_pairs={{0,1},{1,0},{2,3},{3,2},{4,5},{5,4},{6,7},{7,6},{8,9},{9,8},{10,11... | collective-permute-start | bytes 258056 | tf_op jit(solution)/shard_map/ppermute | solution.py:12
  144.4 12.8 %all-to-all-start.2 = ((bf16[12,2,896]{2,1,0:T(2,128)(2,1)}), bf16[12,2,896]{2,1,0:T(2,128)(2,1)S(1)}, u32[]{:S(2)}, u32[]{:S(2)}) async-start(bf16[12,2,896]{2,1,0:T(2,128)(2,1)} %reshape.239), calls=%async_computation.2 | async-start | bytes 86016 | tf_op jit(solution)/shard_map/all_to_all | solution.py:90
  158.5 18.2 %all-to-all-start.3 = ((bf16[64,2,168]{2,1,0:T(2,128)(2,1)}), bf16[64,2,168]{2,1,0:T(2,128)(2,1)S(1)}, u32[]{:S(2)}, u32[]{:S(2)}) async-start(bf16[64,2,168]{2,1,0:T(2,128)(2,1)} %reshape.241), calls=%async_computation.3 | async-start | bytes 131072 | tf_op jit(solution)/shard_map/all_to_all | solution.py:89
where the time goes:
time: 185 us; the launch traced here: 184 us
  waiting for transfers between devices  60.5 us (33%)
  blocking collectives  51.2 us (28%)
  local copies, waits for them, and re-layouts  38.6 us (21%)
  starting transfers between devices  30.1 us (16%)
  other arithmetic  2.02 us (1%)
    ppermute x5, waiting for transfers between devices, from_partner(): lax.ppermute(x, axis, [(i, i ^ 1 << distance) for i in range(lax.axis_siz...  41.4 us
    all_to_all x1, blocking collectives, shards(): lax.all_to_all(widened, 'loc', split_axis=2, concat_axis=2, tiled=True)  26 us
    all_to_all x1, blocking collectives, shards(): lax.all_to_all(outgoing, 'grp', split_axis=0, concat_axis=0, tiled=True)  25.2 us
    ppermute x5, starting transfers between devices, from_partner(): lax.ppermute(x, axis, [(i, i ^ 1 << distance) for i in range(lax.axis_siz...  18.2 us
    unnamed x18, local copies, waits for them, and re-layouts  13.7 us
    all_to_all x1, waiting for transfers between devices, shards(): lax.all_to_all(lax.all_to_all(finished, 'grp', split_axis=0, concat_axis=...  9.77 us
    all_to_all x1, waiting for transfers between devices, shards(): lax.all_to_all(finished, 'grp', split_axis=0, concat_axis=0, tiled=True)  9.32 us
    gather x5, local copies, waits for them, and re-layouts, bin_layout(): slot_index = jnp.take_along_axis(earlier, expert_ids, axis=1)  8.91 us
  transfers between devices with their start and end apart: 7, of which 7 were waited for; matrix products, arithmetic and copies ran while one was open for 0% of the time, Pallas kernels for 0%

commit v1 on v0

v1 whole, which is shorter than its diff:
```python
import jax
import jax.numpy as jnp
from jax import lax
from jax.experimental import pallas as pl
from jax.experimental.pallas import tpu as pltpu
from jax.sharding import PartitionSpec as P

MESH = pl.DeviceIdType.MESH
BF = jnp.bfloat16
F32 = jnp.float32

GROUPS = 12
CHIPS = 32
LINE = 8
SUB = 28
CAP = 8
QUAD = 4
PART = 24


def iota(shape, dim):
    return lax.broadcasted_iota(jnp.int32, shape, dim)


def onehot(condition):
    return jnp.where(condition, 1.0, 0.0).astype(BF)


def dot(a, b):
    return jnp.dot(a, b, preferred_element_type=F32)


def dot_nt(a, b):
    return lax.dot_general(a, b, (((1,), (1,)), ((), ())), preferred_element_type=F32)


def block_transpose(v):
    lane = iota(v[0].shape, 1)
    low64 = lane < 64
    low32 = (lane & 32) == 0
    t = [None] * 4
    for a in range(2):
        t[a] = jnp.where(low64, v[a], pltpu.roll(v[a + 2], 64, 1))
        t[a + 2] = jnp.where(low64, pltpu.roll(v[a], 64, 1), v[a + 2])
    w = [None] * 4
    for a in (0, 2):
        w[a] = jnp.where(low32, t[a], pltpu.roll(t[a + 1], 32, 1))
        w[a + 1] = jnp.where(low32, pltpu.roll(t[a], 96, 1), t[a + 1])
    return w


def send(src, dst, send_sem, recv_sem, device):
    pltpu.make_async_remote_copy(
        src_ref=src,
        dst_ref=dst,
        send_sem=send_sem,
        recv_sem=recv_sem,
        device_id=device,
        device_id_type=MESH,
    ).start()


def wait_bytes(ref, sem):
    pltpu.make_async_copy(ref, ref, sem).wait()


def expert_of(b):
    return ((b >> 4) * 16 + ((b >> 3) & 1)).astype(F32)


def kernel(
    tok_ref, ids_ref, gw_ref, wg_hbm, wu_hbm, wd_hbm, out_ref,
    wg, wu, wd, wp, dp, tmat, wt, abuf, r1, pbuf, x2, actf, gs, gr, hb,
    yb, yr, cs, r3, dbuf, r4,
    wsem, a_s, a_r, p_s, p_r, f_s, f_r, g_s, g_r, h_s, h_r, y_s, y_r, c_s, c_r, d_s, d_r,
):
    z = lax.axis_index("grp")
    l = lax.axis_index("loc")
    chip = lax.div(l, 2)
    c = lax.rem(l, 2)
    other = 1 - c
    x = lax.div(chip, LINE)
    y = lax.rem(chip, LINE)
    partner = (z, 2 * chip + other)

    loads = [
        pltpu.make_async_copy(src.at[0], dst, wsem.at[i])
        for i, (src, dst) in enumerate(((wg_hbm, wg), (wu_hbm, wu), (wd_hbm, wd)))
    ]
    for copy in loads:
        copy.start()

    barrier = pltpu.get_barrier_semaphore()

    def hello_grp(k, carry):
        pl.semaphore_signal(
            barrier, inc=1, device_id=(lax.rem(z + k, GROUPS), l), device_id_type=MESH
        )
        return carry

    lax.fori_loop(1, GROUPS, hello_grp, 0)

    def hello_loc(k, carry):
        there = lax.rem(chip + k, CHIPS)
        pl.semaphore_signal(barrier, inc=1, device_id=(z, 2 * there + c), device_id_type=MESH)
        return carry

    lax.fori_loop(1, CHIPS, hello_loc, 0)
    pl.semaphore_signal(barrier, inc=1, device_id=partner, device_id_type=MESH)

    abuf[...] = jnp.zeros(abuf.shape, BF)
    ids = ids_ref[...].astype(F32)
    eye = onehot(iota((8, 8), 0) == iota((8, 8), 1))
    ids_t = dot_nt(eye, ids.astype(BF))
    bins = GROUPS * 16
    b = iota((bins, 128), 0)
    e_b = expert_of(b)
    hit = ids_t[0:1, :] == e_b
    for k in range(1, 8):
        hit = hit | (ids_t[k : k + 1, :] == e_b)
    before = onehot(iota((128, 128), 0) < iota((128, 128), 1))
    earlier = dot(onehot(hit), before)
    selector = onehot(hit & (earlier == (b & 7).astype(F32)))
    rows = dot(selector, tok_ref[...])
    abuf[:, :, 0:112] = rows.astype(BF).reshape(GROUPS, 16, 112)

    pl.semaphore_wait(barrier, GROUPS - 1 + CHIPS - 1 + 1)

    def send_a(k, carry):
        g = lax.rem(z + k, GROUPS)
        send(abuf.at[g], r1.at[z], a_s, a_r, (g, l))
        return carry

    lax.fori_loop(1, GROUPS, send_a, 0)
    r1[pl.ds(z, 1)] = abuf[pl.ds(z, 1)]

    i = iota((128, 512), 0)
    n = iota((128, 512), 1)
    match = ((n & 31) < SUB) & (i == (n >> 7) * SUB + (n & 31))
    for r in range(QUAD):
        tmat[128 * r : 128 * (r + 1), :] = onehot(match & (((n >> 5) & 3) == r))

    loads[0].wait()
    loads[1].wait()
    i = iota((128, 112), 0)
    widen = onehot(((i & 31) < SUB) & (iota((128, 112), 1) == (i >> 5) * SUB + (i & 31)))

    def widen_in(m, carry):
        src = pl.ds(pl.multiple_of(112 * m, 16), 112)
        dst = pl.ds(pl.multiple_of(128 * lax.rem(m, 4), 128), 128)
        k = lax.div(m, 4)
        wp[k, dst, 0:256] = dot(widen, wg[src, :]).astype(BF)
        wp[k, dst, 256:512] = dot(widen, wu[src, :]).astype(BF)
        return carry

    lax.fori_loop(0, 16, widen_in, 0)

    wait_bytes(r1.at[pl.ds(0, GROUPS - 1)], a_r)
    arrived = r1[...].astype(F32)
    left = []
    for j in range(2):
        mine = arrived[:, 8 * j : 8 * j + 8, :].reshape(QUAD, PART, 128)
        left.append(jnp.concatenate([mine[r] for r in range(QUAD)], axis=1))
    packed = dot(jnp.concatenate(left, axis=0).astype(BF), tmat[...])
    for j in range(2):
        for q in range(QUAD):
            pbuf[QUAD * j + q] = packed[PART * j : PART * (j + 1), 128 * q : 128 * (q + 1)].astype(BF)

    def send_p(k, carry):
        d = lax.div(k, LINE)
        there = LINE * lax.rem(x + d, 4) + lax.rem(y + lax.rem(k, LINE), LINE)
        send(
            pbuf.at[lax.div(there, 4)], x2.at[c, chip], p_s, p_r.at[d], (z, 2 * there + c)
        )
        return carry

    lax.fori_loop(1, CHIPS, send_p, 0)
    x2[pl.ds(c, 1), pl.ds(chip, 1)] = pbuf[pl.ds(lax.div(chip, 4), 1)].reshape(1, 1, PART, 128)

    e_row = expert_of(iota((128, bins), 1))
    gate = gw_ref[...]
    same = jnp.zeros((128, bins), F32)
    weight = jnp.zeros((128, bins), F32)
    for k in range(8):
        eq = ids[:, k : k + 1] == e_row
        same = jnp.where(eq, 1.0, same)
        weight = jnp.where(eq, gate[:, k : k + 1], weight)
    after = onehot(iota((128, 128), 1) < iota((128, 128), 0))
    slot = dot(after, same.astype(BF))
    weight = jnp.where(slot == (iota((128, bins), 1) & 7).astype(F32), weight, 0.0)
    high = weight.astype(BF)
    wt[0] = high
    wt[1] = (weight - high.astype(F32)).astype(BF)

    loads[2].wait()
    for m in range(16):
        first = 112 * m // 128
        off = 112 * m - 128 * first
        width = 128 if off <= 16 else 256
        i = iota((width, 128), 0)
        n = iota((width, 128), 1)
        spread = onehot(((n & 31) < SUB) & (i == off + (n >> 5) * SUB + (n & 31)))
        dp[m // 4, :, 128 * (m % 4) : 128 * (m % 4 + 1)] = dot(
            wd[:, 128 * first : 128 * first + width], spread
        ).astype(BF)

    total = jnp.zeros((4 * PART, 512), F32)
    for step in range(5):
        if step < 4:
            ch = pl.ds(LINE * lax.rem(x + 4 - step, 4), LINE)
            wait_bytes(x2.at[0, pl.ds(0, LINE - 1 if step == 0 else LINE)], p_r.at[step])
            send(x2.at[c, ch], x2.at[c, ch], f_s, f_r.at[step], partner)
        if step >= 1:
            k = lax.rem(x + 5 - step, 4)
            wait_bytes(x2.at[0, pl.ds(0, LINE)], f_r.at[step - 1])
            half = [x2[p, pl.ds(LINE * k, LINE)].astype(F32) for p in range(2)]
            cols = []
            for m in range(4):
                w = block_transpose([half[a % 2][2 * m + a // 2] for a in range(4)])
                cols.append(jnp.concatenate(w, axis=0).astype(BF))
            total = total + dot(jnp.concatenate(cols, axis=1), wp[k])
    act = total.reshape(4, PART, 512)
    actf[...] = act
    gs[...] = act.astype(BF)

    q = 2 * lax.rem(x, 2) + lax.div(y, 4)

    def mate(qq):
        there = LINE * (2 * lax.div(x, 2) + lax.div(qq, 2)) + 4 * lax.rem(qq, 2) + lax.rem(y, 4)
        return (z, 2 * there + c)

    for k in range(1, 4):
        qq = lax.rem(q + k, 4)
        send(gs.at[qq], gr.at[q], g_s, g_r, mate(qq))
    wait_bytes(gr.at[pl.ds(0, 3)], g_r)
    summed = actf[q]
    for k in range(1, 4):
        summed = summed + gr[lax.rem(q + k, 4)].astype(F32)
    gate_act = summed[:, 0:256]
    hidden = gate_act * (1.0 / (1.0 + jnp.exp(-gate_act))) * summed[:, 256:512]
    hb[q] = hidden.astype(BF)
    for k in range(1, 4):
        send(hb.at[q], hb.at[q], h_s, h_r, mate(lax.rem(q + k, 4)))
    wait_bytes(hb.at[pl.ds(0, 3)], h_r)
    hid = hb[...].astype(F32).reshape(4 * PART, 256).astype(BF)

    for step in range(4):
        k = lax.rem(x + step, 4)
        part = dot(hid, dp[k])
        for m in range(4):
            w = block_transpose(
                [part[PART * r : PART * (r + 1), 128 * m : 128 * (m + 1)] for r in range(4)]
            )
            for a in range(4):
                yb[a % 2, LINE * k + 2 * m + a // 2] = w[a].astype(BF)
        ch = pl.ds(LINE * k, LINE)
        send(yb.at[other, ch], yr.at[ch], y_s, y_r.at[step], partner)
    for step in range(4):
        k = lax.rem(x + step, 4)
        ch = pl.ds(LINE * k, LINE)
        wait_bytes(yr.at[ch], y_r.at[step])
        cs[ch] = (yb[c, ch].astype(F32) + yr[ch].astype(F32)).astype(BF)

        def send_c(o, carry, k=k):
            there = LINE * k + lax.rem(y + o, LINE)
            send(cs.at[there], r3.at[chip], c_s, c_r, (z, 2 * there + c))
            return carry

        lax.fori_loop(1 if step == 0 else 0, LINE, send_c, 0)
        if step == 0:
            r3[pl.ds(chip, 1)] = cs[pl.ds(chip, 1)]

    wait_bytes(r3.at[pl.ds(0, CHIPS - 1)], c_r)
    parts = r3[...].astype(F32).reshape(8, 4, PART, 128)
    done = parts[:, 0] + parts[:, 1] + parts[:, 2] + parts[:, 3]
    left = [
        jnp.concatenate([done[QUAD * j + qq] for qq in range(QUAD)], axis=1) for j in range(2)
    ]
    laid = dot_nt(jnp.concatenate(left, axis=0).astype(BF), tmat[...])
    for s in range(GROUPS):
        r, k = s // 3, s % 3
        dbuf[s] = jnp.concatenate(
            [
                laid[PART * j + 8 * k : PART * j + 8 * k + 8, 128 * r : 128 * (r + 1)]
                for j in range(2)
            ],
            axis=0,
        ).astype(BF)

    def send_d(k, carry):
        s = lax.rem(z + k, GROUPS)
        send(dbuf.at[s], r4.at[z], d_s, d_r, (s, l))
        return carry

    lax.fori_loop(1, GROUPS, send_d, 0)
    r4[pl.ds(z, 1)] = dbuf[pl.ds(z, 1)]
    wait_bytes(r4.at[pl.ds(0, GROUPS - 1)], d_r)
    back = r4[...].reshape(bins, 128)
    combined = dot(wt[0], back) + dot(wt[1], back)
    out_ref[...] = combined[:, 0:112].astype(BF)

    wait_bytes(abuf.at[pl.ds(0, GROUPS - 1)], a_s)
    wait_bytes(x2.at[0, pl.ds(0, CHIPS - 1)], p_s)
    wait_bytes(x2.at[0], f_s)
    wait_bytes(gs.at[pl.ds(0, 3)], g_s)
    wait_bytes(hb.at[pl.ds(0, 3)], h_s)
    wait_bytes(yr, y_s)
    wait_bytes(cs.at[pl.ds(0, CHIPS - 1)], c_s)
    wait_bytes(dbuf.at[pl.ds(0, GROUPS - 1)], d_s)


def shards(tokens, expert_ids, gate_weights, gate_blocks, up_blocks, down_blocks):
    vmem = pl.BlockSpec(memory_space=pltpu.VMEM)
    hbm = pl.BlockSpec(memory_space=pl.ANY)
    dma = pltpu.SemaphoreType.DMA
    return pl.pallas_call(
        kernel,
        out_shape=jax.ShapeDtypeStruct(tokens.shape, BF),
        in_specs=[vmem, vmem, vmem, hbm, hbm, hbm],
        out_specs=vmem,
        scratch_shapes=[
            pltpu.VMEM((1792, 256), BF),
            pltpu.VMEM((1792, 256), BF),
            pltpu.VMEM((256, 1792), BF),
            pltpu.VMEM((4, 512, 512), BF),
            pltpu.VMEM((4, 256, 512), BF),
            pltpu.VMEM((512, 512), BF),
            pltpu.VMEM((2, 128, 192), BF),
            pltpu.VMEM((GROUPS, 16, 128), BF),
            pltpu.VMEM((GROUPS, 16, 128), BF),
            pltpu.VMEM((8, PART, 128), BF),
            pltpu.VMEM((2, CHIPS, PART, 128), BF),
            pltpu.VMEM((4, PART, 512), F32),
            pltpu.VMEM((4, PART, 512), BF),
            pltpu.VMEM((4, PART, 512), BF),
            pltpu.VMEM((4, PART, 256), BF),
            pltpu.VMEM((2, CHIPS, PART, 128), BF),
            pltpu.VMEM((CHIPS, PART, 128), BF),
            pltpu.VMEM((CHIPS, PART, 128), BF),
            pltpu.VMEM((CHIPS, PART, 128), BF),
            pltpu.VMEM((GROUPS, 16, 128), BF),
            pltpu.VMEM((GROUPS, 16, 128), BF),
            dma((3,)),
            dma, dma,
            dma, dma((4,)),
            dma, dma((4,)),
            dma, dma,
            dma, dma,
            dma, dma((4,)),
            dma, dma,
            dma, dma,
        ],
        compiler_params=pltpu.CompilerParams(
            collective_id=0, has_side_effects=True, vmem_limit_bytes=40 * 1024 * 1024
        ),
        name="moe_layer",
    )(tokens, expert_ids, gate_weights, gate_blocks, up_blocks, down_blocks)


def solution(mesh):
    in_specs = (
        P("grp", "loc"),
        P("grp", None),
        P("grp", None),
        P(("grp", "loc"), None, None),
        P(("grp", "loc"), None, None),
        P(("grp", "loc"), None, None),
    )
    return jax.shard_map(
        shards, mesh=mesh, in_specs=in_specs, out_specs=P("grp", "loc"), check_vma=False
    )
```

time: 185 us -> 69.1 us (0.37)
  Pallas kernels: 0 us -> 62.7 us
  waiting for transfers between devices: 60.5 us -> 0 us
  blocking collectives: 51.2 us -> 0 us
  local copies, waits for them, and re-layouts: 38.6 us -> 5.9 us
  starting transfers between devices: 30.1 us -> 0 us
  other arithmetic: 2.02 us -> 0 us
    pallas_call x0 -> x1, Pallas kernels: none -> 62.7 us  [shards(): pl.pallas_call(kernel, out_shape=jax.ShapeDtypeStruct(tokens.shape, BF),...]
    all_to_all x2 -> x0, blocking collectives: 51.2 us -> none  [the longest x1 26 us: shards(): lax.all_to_all(widened, 'loc', split_axis=2, concat_axis=2, tiled=True)]
    ppermute x5 -> x0, waiting for transfers between devices: 41.4 us -> none  [from_partner(): lax.ppermute(x, axis, [(i, i ^ 1 << distance) for i in range(lax.axis_siz...]
    all_to_all x2 -> x0, waiting for transfers between devices: 19.1 us -> none  [the longest x1 9.77 us: shards(): lax.all_to_all(lax.all_to_all(finished, 'grp', split_axis=0, concat_axis=...]
    ppermute x5 -> x0, starting transfers between devices: 18.2 us -> none  [from_partner(): lax.ppermute(x, axis, [(i, i ^ 1 << distance) for i in range(lax.axis_siz...]
    gather x13 -> x0, local copies, waits for them, and re-layouts: 14.6 us -> none  [the longest x5 8.91 us: bin_layout(): slot_index = jnp.take_along_axis(earlier, expert_ids, axis=1)]
    all_to_all x2 -> x0, starting transfers between devices: 11.9 us -> none  [the longest x1 8.42 us: shards(): lax.all_to_all(lax.all_to_all(finished, 'grp', split_axis=0, concat_axis=...]
    unnamed x18 -> x13, local copies, waits for them, and re-layouts: 13.7 us -> 5.18 us
  transfers between devices with their start and end apart: 7 -> 0, of which waited for: 7 -> 0; matrix products, arithmetic and copies ran while one was open for 0% -> 0% of each run, Pallas kernels for 0% -> 0%
where the time goes in v1:
time: 69.1 us; the launch traced here: 68.6 us
  Pallas kernels  62.7 us (91%)
  local copies, waits for them, and re-layouts  5.9 us (9%)
    pallas_call x1, Pallas kernels, shards(): pl.pallas_call(kernel, out_shape=jax.ShapeDtypeStruct(tokens.shape, BF),...  62.7 us
    unnamed x13, local copies, waits for them, and re-layouts  5.18 us

profile of v1, /device:TPU:1, one launch (start us, length us, event | category | flops | bytes accessed | tf_op | source)
XLA Modules:
  0.0 68.6 jit_solution(4555155970307694181)
XLA Ops:
  0.0 0.0 copy-start.3
  0.0 0.9 %copy.7.tok_ref = bf16[128,112]{1,0:T(8,128)(2,1)S(1)} copy(bf16[128,112]{0,1:T(8,128)(2,1)} %param.6) | data formatting | bytes 57344 | tf_op args[0]
  0.9 0.0 copy-done.3
  0.9 0.0 copy-start.4
  0.9 0.1 copy.8.ids_ref
  1.0 0.6 copy-done.4
  1.6 0.1 copy.9.gw_ref
  1.7 0.0 copy-start
  1.7 1.2 %copy-done = bf16[1,1792,256]{2,1,0:T(8,128)(2,1)S(1)} copy-done((bf16[1,1792,256]{2,1,0:T(8,128)(2,1)S(1)}, bf16[1,1792,256]{2,1,0:T(8,128)(2,1)}, u32[]{:S(2)}) %copy-start) | copy-done | bytes 917528
  2.9 0.0 copy-start.1
  2.9 1.2 %copy-done.1 = bf16[1,1792,256]{2,1,0:T(8,128)(2,1)S(1)} copy-done((bf16[1,1792,256]{2,1,0:T(8,128)(2,1)S(1)}, bf16[1,1792,256]{2,1,0:T(8,128)(2,1)}, u32[]{:S(2)}) %copy-start.1) | copy-done | bytes 917528
  4.0 0.0 copy-start.2
  4.0 1.2 %copy-done.2 = bf16[1,256,1792]{2,1,0:T(8,128)(2,1)S(1)} copy-done((bf16[1,256,1792]{2,1,0:T(8,128)(2,1)S(1)}, bf16[1,256,1792]{2,1,0:T(8,128)(2,1)}, u32[]{:S(2)}) %copy-start.2) | copy-done | bytes 917528
  5.2 62.7 %moe_layer.1 = bf16[128,112]{1,0:T(8,128)(2,1)S(1)} custom-call(bf16[128,112]{1,0:T(8,128)(2,1)S(1)} %copy.7.tok_ref, s32[128,8]{1,0:T(8,128)S(1)} %copy.8.ids_ref, f32[128,8]{1,0:T(8,128)S(1)} %copy.9.gw_ref, bf16[1,1792,256]{2,1,0:T(8,128)(2,1)S(1)} %copy-done, bf16[1,1792,256]{2,1,0:T(8,128)(2,1)S(1)} %copy-done.1, bf16[1,256,1792]{2,1,0:T(8,128)(2,1)S(1)} %copy-done.2), custom_call_target="tpu_custom_call" | custom-call | tf_op jit(solution)/shard_map/moe_layer/pallas_call | solution.py:316
  67.9 0.7 %copy.10 = bf16[128,112]{0,1:T(8,128)(2,1)} copy(bf16[128,112]{1,0:T(8,128)(2,1)S(1)} %moe_layer.1) | data formatting | bytes 57344 | tf_op jit(solution)/shard_map/moe_layer/pallas_call | solution.py:316
Async XLA Ops:
  0.0 0.9 %copy-start.3 = (s32[128,8]{0,1:T(8,128)S(1)}, s32[128,8]{0,1:T(8,128)}, u32[]{:S(2)}) copy-start(s32[128,8]{0,1:T(8,128)} %param.7) | copy-start | bytes 12292
  0.9 0.7 %copy-start.4 = (f32[128,8]{0,1:T(8,128)S(1)}, f32[128,8]{0,1:T(8,128)}, u32[]{:S(2)}) copy-start(f32[128,8]{0,1:T(8,128)} %param.8) | copy-start | bytes 12292
  1.7 1.2 %copy-start = (bf16[1,1792,256]{2,1,0:T(8,128)(2,1)S(1)}, bf16[1,1792,256]{2,1,0:T(8,128)(2,1)}, u32[]{:S(2)}) copy-start(bf16[1,1792,256]{2,1,0:T(8,128)(2,1)} %wg_hbm.1) | copy-start | bytes 2752516
  2.9 1.2 %copy-start.1 = (bf16[1,1792,256]{2,1,0:T(8,128)(2,1)S(1)}, bf16[1,1792,256]{2,1,0:T(8,128)(2,1)}, u32[]{:S(2)}) copy-start(bf16[1,1792,256]{2,1,0:T(8,128)(2,1)} %wu_hbm.1) | copy-start | bytes 2752516
  4.0 1.2 %copy-start.2 = (bf16[1,256,1792]{2,1,0:T(8,128)(2,1)S(1)}, bf16[1,256,1792]{2,1,0:T(8,128)(2,1)}, u32[]{:S(2)}) copy-start(bf16[1,256,1792]{2,1,0:T(8,128)(2,1)} %wd_hbm.1) | copy-start | bytes 2752516

commit v2 on v0

v2 whole, which is shorter than its diff:
```python
import jax
import jax.numpy as jnp
from jax import lax
from jax.experimental import pallas as pl
from jax.experimental.pallas import tpu as pltpu
from jax.sharding import PartitionSpec as P

MESH = pl.DeviceIdType.MESH
BF = jnp.bfloat16
F32 = jnp.float32

GROUPS = 12
CHIPS = 32
LINE = 8
SUB = 28
QUAD = 4
BINS = GROUPS * 16
CHUNKS = ((0, 1), (1, 1), (2, 1))


def iota(shape, dim):
    return lax.broadcasted_iota(jnp.int32, shape, dim)


def onehot(condition):
    return jnp.where(condition, 1.0, 0.0).astype(BF)


def dot(a, b, dims=((1,), (0,))):
    return lax.dot_general(a, b, (dims, ((), ())), preferred_element_type=F32)


def offset(n):
    return lax.div(n + 1, 2) * (1 - 2 * lax.rem(n + 1, 2))


def block_transpose(v):
    lane = iota(v[0].shape, 1)
    low64 = lane < 64
    low32 = (lane & 32) == 0
    t = [None] * 4
    for a in range(2):
        t[a] = jnp.where(low64, v[a], pltpu.roll(v[a + 2], 64, 1))
        t[a + 2] = jnp.where(low64, pltpu.roll(v[a], 64, 1), v[a + 2])
    w = [None] * 4
    for a in (0, 2):
        w[a] = jnp.where(low32, t[a], pltpu.roll(t[a + 1], 32, 1))
        w[a + 1] = jnp.where(low32, pltpu.roll(t[a], 96, 1), t[a + 1])
    return w


def send(src, dst, send_sem, recv_sem, device):
    pltpu.make_async_remote_copy(
        src_ref=src,
        dst_ref=dst,
        send_sem=send_sem,
        recv_sem=recv_sem,
        device_id=device,
        device_id_type=MESH,
    ).start()


def wait_bytes(ref, sem):
    pltpu.make_async_copy(ref, ref, sem).wait()


def kernel(
    tok_hbm, ids_hbm, gw_hbm, wg_hbm, wu_hbm, wd_hbm, out_ref,
    tok, ids_v, gw, wg, wu, wd, wp, dp, tmat, wt, abuf, r1, dbuf, r4, chunk_bufs,
    load_sem, a_s, a_r, d_s, d_r, chunk_s, chunk_r,
):
    z = lax.axis_index("grp")
    l = lax.axis_index("loc")
    chip = lax.div(l, 2)
    c = lax.rem(l, 2)
    other = 1 - c
    x = lax.div(chip, LINE)
    y = lax.rem(chip, LINE)
    partner = (z, 2 * chip + other)

    def far_first(i):
        xx = lax.rem(x + 6 + offset(lax.rem(i, 4)), 4)
        yy = lax.rem(y + 12 + offset(lax.div(i, 4)), LINE)
        return LINE * xx + yy

    barrier = pltpu.get_barrier_semaphore()

    def hello_grp(i, carry):
        there = lax.rem(z + GROUPS + offset(GROUPS - 1 - i), GROUPS)
        pl.semaphore_signal(barrier, inc=1, device_id=(there, l), device_id_type=MESH)
        return carry

    lax.fori_loop(0, GROUPS - 1, hello_grp, 0)

    loads = [
        pltpu.make_async_copy(src, dst, load_sem.at[i])
        for i, (src, dst) in enumerate(
            (
                (tok_hbm, tok), (ids_hbm, ids_v), (gw_hbm, gw),
                (wg_hbm.at[0], wg), (wu_hbm.at[0], wu), (wd_hbm.at[0], wd),
            )
        )
    ]
    for copy in loads:
        copy.start()

    def hello_loc(i, carry):
        pl.semaphore_signal(
            barrier, inc=1, device_id=(z, 2 * far_first(i) + c), device_id_type=MESH
        )
        return carry

    lax.fori_loop(0, CHIPS - 1, hello_loc, 0)
    pl.semaphore_signal(barrier, inc=1, device_id=partner, device_id_type=MESH)

    abuf[...] = jnp.zeros(abuf.shape, BF)
    b = iota((BINS, 128), 0)
    n = b >> 4
    half = (n + 1) >> 1
    there = z - jnp.where((n & 1) == 1, half, -half)
    there = jnp.where(there < 0, there + GROUPS, there)
    there = jnp.where(there >= GROUPS, there - GROUPS, there)
    e_b = there * 16 + ((b >> 3) & 1)
    before = onehot(iota((128, 128), 0) < iota((128, 128), 1))
    for copy in loads[:3]:
        copy.wait()
    ids = ids_v[...]
    hit = ids[0:1, :] == e_b
    for k in range(1, 8):
        hit = hit | (ids[k : k + 1, :] == e_b)
    earlier = dot(onehot(hit), before)
    kept = hit & (earlier == (b & 7).astype(F32))
    rows = dot(onehot(kept), tok[...], ((1,), (1,)))
    abuf[:, :, 0:112] = rows.astype(BF).reshape(GROUPS, 16, 112)

    weight = jnp.zeros((BINS, 128), F32)
    for k in range(8):
        weight = jnp.where(ids[k : k + 1, :] == e_b, gw[k : k + 1, :], weight)
    weight = jnp.where(kept, weight, 0.0)
    high = weight.astype(BF)
    wt[0] = high
    wt[1] = (weight - high.astype(F32)).astype(BF)

    i = iota((128, 512), 0)
    n = iota((128, 512), 1)
    match = ((n & 31) < SUB) & (i == (n >> 7) * SUB + (n & 31))
    for r in range(QUAD):
        tmat[128 * r : 128 * (r + 1), :] = onehot(match & (((n >> 5) & 3) == r))

    pl.semaphore_wait(barrier, GROUPS - 1 + CHIPS - 1 + 1)

    for t, (first, fours) in reversed(list(enumerate(CHUNKS))):
        low, high = max(1, 4 * first), 4 * (first + fours)

        def send_a(i, carry, t=t, high=high):
            s = high - 1 - i
            g = lax.rem(z + GROUPS - offset(s), GROUPS)
            send(abuf.at[s], r1.at[s], a_s, a_r.at[t], (g, l))
            return carry

        lax.fori_loop(0, high - low, send_a, 0)
    r1[0] = abuf[0]

    loads[3].wait()
    loads[4].wait()
    i = iota((128, 112), 0)
    widen = onehot(((i & 31) < SUB) & (iota((128, 112), 1) == (i >> 5) * SUB + (i & 31)))
    for m in range(16):
        src, dst = pl.ds(112 * m, 112), pl.ds(128 * m, 128)
        wp[dst, 0:256] = dot(widen, wg[src, :]).astype(BF)
        wp[dst, 256:512] = dot(widen, wu[src, :]).astype(BF)
    loads[5].wait()
    for m in range(16):
        first = 112 * m // 128
        off = 112 * m - 128 * first
        width = 128 if off <= 16 else 256
        i = iota((width, 128), 0)
        n = iota((width, 128), 1)
        spread = onehot(((n & 31) < SUB) & (i == off + (n >> 5) * SUB + (n & 31)))
        dp[:, 128 * m : 128 * (m + 1)] = dot(wd[:, 128 * first : 128 * first + width], spread).astype(BF)

    q = 2 * lax.rem(x, 2) + lax.div(y, 4)

    def mate(k):
        qq = lax.rem(q + k, 4)
        there = LINE * (2 * lax.div(x, 2) + lax.div(qq, 2)) + 4 * lax.rem(qq, 2) + lax.rem(y, 4)
        return (z, 2 * there + c)

    A, PK, F, G, Y, C = range(6)

    def pack(t):
        first, fours = CHUNKS[t]
        pbuf, x2 = chunk_bufs[t][0:2]
        width = 8 * fours
        wait_bytes(r1.at[pl.ds(0, 4 * fours - (1 if first == 0 else 0))], a_r.at[t])
        came = r1[4 * first : 4 * (first + fours)].astype(F32).reshape(fours, QUAD, 16, 128)
        left = [
            jnp.concatenate(
                [came[:, r, 8 * j : 8 * j + 8, :].reshape(width, 128) for r in range(QUAD)], axis=1
            )
            for j in range(2)
        ]
        packed = dot(jnp.concatenate(left, axis=0).astype(BF), tmat[...])
        for j in range(2):
            for qq in range(QUAD):
                pbuf[QUAD * j + qq] = packed[
                    width * j : width * (j + 1), 128 * qq : 128 * (qq + 1)
                ].astype(BF)

        def send_p(i, carry):
            there = far_first(i)
            send(
                pbuf.at[lax.div(there, 4)], x2.at[c, chip], chunk_s.at[t, PK], chunk_r.at[t, PK],
                (z, 2 * there + c),
            )
            return carry

        lax.fori_loop(0, CHIPS - 1, send_p, 0)
        x2[pl.ds(c, 1), pl.ds(chip, 1)] = pbuf[pl.ds(lax.div(chip, 4), 1)].reshape(1, 1, width, 128)

    def forward(t):
        x2 = chunk_bufs[t][1]
        wait_bytes(x2.at[0, pl.ds(0, CHIPS - 1)], chunk_r.at[t, PK])
        send(x2.at[c], x2.at[c], chunk_s.at[t, F], chunk_r.at[t, F], partner)

    def gate_up(t):
        x2, actf, gs, gr = chunk_bufs[t][1:5]
        width = 8 * CHUNKS[t][1]
        wait_bytes(x2.at[0], chunk_r.at[t, F])
        both = [x2[p].astype(F32).reshape(16, 2, width, 128) for p in range(2)]
        w = block_transpose([both[a % 2][:, a // 2].reshape(16 * width, 128) for a in range(4)])
        w = [v.reshape(16, width, 128) for v in w]
        cols = [jnp.concatenate([w[r][m] for r in range(4)], axis=0).astype(BF) for m in range(16)]
        act = dot(jnp.concatenate(cols, axis=1), wp[...])
        actf[...] = act
        gs[...] = act.astype(BF)
        for k in (3, 1, 2):
            send(gs, gr.at[k - 1], chunk_s.at[t, G], chunk_r.at[t, G], mate(k))

    def down(t):
        actf, gs, gr, yb, yr = chunk_bufs[t][2:7]
        width = 8 * CHUNKS[t][1]
        wait_bytes(gr, chunk_r.at[t, G])
        act = actf[...]
        for k in range(3):
            act = act + gr[k].astype(F32)
        gate = act[:, 0:256]
        hidden = (gate * (1.0 / (1.0 + jnp.exp(-gate))) * act[:, 256:512]).astype(BF)
        part = dot(hidden, dp[...])
        w = block_transpose(
            [
                jnp.concatenate(
                    [
                        part[width * r : width * (r + 1), 128 * m : 128 * (m + 1)]
                        for m in range(16)
                    ],
                    axis=0,
                )
                for r in range(4)
            ]
        )
        for a in range(4):
            yb[a % 2, :, a // 2] = w[a].astype(BF).reshape(16, width, 128)
        send(yb.at[other], yr, chunk_s.at[t, Y], chunk_r.at[t, Y], partner)

    def spread_out(t):
        yb, yr, cs, r3 = chunk_bufs[t][5:9]
        width = 8 * CHUNKS[t][1]
        wait_bytes(yr, chunk_r.at[t, Y])
        cs[...] = (yb[c].astype(F32) + yr[...].astype(F32)).astype(BF).reshape(CHIPS, width, 128)

        def send_c(i, carry):
            there = far_first(i)
            send(
                cs.at[there], r3.at[chip], chunk_s.at[t, C], chunk_r.at[t, C], (z, 2 * there + c)
            )
            return carry

        lax.fori_loop(0, CHIPS - 1, send_c, 0)
        r3[pl.ds(chip, 1)] = cs[pl.ds(chip, 1)]

    def home(t):
        first, fours = CHUNKS[t]
        r3 = chunk_bufs[t][8]
        width = 8 * fours
        wait_bytes(r3.at[pl.ds(0, CHIPS - 1)], chunk_r.at[t, C])
        parts = r3[...].astype(F32).reshape(8, 4, width, 128)
        done = parts[:, 0] + parts[:, 1] + parts[:, 2] + parts[:, 3]
        left = [
            jnp.concatenate([done[QUAD * j + qq] for qq in range(QUAD)], axis=1) for j in range(2)
        ]
        laid = dot(jnp.concatenate(left, axis=0).astype(BF), tmat[...], ((1,), (1,)))
        for n in range(fours):
            for r in range(QUAD):
                dbuf[4 * (first + n) + r] = jnp.concatenate(
                    [
                        laid[width * j + 8 * n : width * j + 8 * n + 8, 128 * r : 128 * (r + 1)]
                        for j in range(2)
                    ],
                    axis=0,
                ).astype(BF)
        low, high = max(1, 4 * first), 4 * (first + fours)

        def send_d(i, carry):
            s = high - 1 - i
            send(
                dbuf.at[s], r4.at[s], d_s, d_r, (lax.rem(z + GROUPS + offset(s), GROUPS), l)
            )
            return carry

        lax.fori_loop(0, high - low, send_d, 0)

    count = len(CHUNKS)
    for t in range(count):
        pack(t)
    for t in range(count):
        forward(t)
        if t >= 1:
            gate_up(t - 1)
    gate_up(count - 1)
    for t in range(count):
        down(t)
        if t >= 1:
            spread_out(t - 1)
    spread_out(count - 1)
    for t in reversed(range(count)):
        home(t)
    r4[0] = dbuf[0]
    wait_bytes(r4.at[pl.ds(0, GROUPS - 1)], d_r)
    back = r4[...].reshape(BINS, 128)
    combined = dot(back, wt[0], ((0,), (0,))) + dot(back, wt[1], ((0,), (0,)))
    out_ref[...] = combined[0:112, :].astype(BF)

    wait_bytes(abuf.at[pl.ds(0, GROUPS - 1)], a_s)
    wait_bytes(dbuf.at[pl.ds(0, GROUPS - 1)], d_s)
    for t in range(count):
        x2, gr, yr, cs = (chunk_bufs[t][i] for i in (1, 4, 6, 7))
        wait_bytes(x2.at[0, pl.ds(0, CHIPS - 1)], chunk_s.at[t, PK])
        wait_bytes(x2.at[0], chunk_s.at[t, F])
        wait_bytes(gr, chunk_s.at[t, G])
        wait_bytes(yr, chunk_s.at[t, Y])
        wait_bytes(cs.at[pl.ds(0, CHIPS - 1)], chunk_s.at[t, C])


def chunk_scratch(fours):
    width = 8 * fours
    return [
        pltpu.VMEM((8, width, 128), BF),
        pltpu.VMEM((2, CHIPS, width, 128), BF),
        pltpu.VMEM((4 * width, 512), F32),
        pltpu.VMEM((4 * width, 512), BF),
        pltpu.VMEM((3, 4 * width, 512), BF),
        pltpu.VMEM((2, 16, 2, width, 128), BF),
        pltpu.VMEM((16, 2, width, 128), BF),
        pltpu.VMEM((CHIPS, width, 128), BF),
        pltpu.VMEM((CHIPS, width, 128), BF),
    ]


def shards(tokens, expert_ids, gate_weights, gate_blocks, up_blocks, down_blocks):
    hbm = pl.BlockSpec(memory_space=pl.ANY)
    dma = pltpu.SemaphoreType.DMA
    count = len(CHUNKS)
    combined = pl.pallas_call(
        kernel,
        out_shape=jax.ShapeDtypeStruct(tokens.shape[::-1], BF),
        in_specs=[hbm] * 6,
        out_specs=pl.BlockSpec(memory_space=pltpu.VMEM),
        scratch_shapes=[
            pltpu.VMEM((112, 128), BF),
            pltpu.VMEM((8, 128), jnp.int32),
            pltpu.VMEM((8, 128), F32),
            pltpu.VMEM((1792, 256), BF),
            pltpu.VMEM((1792, 256), BF),
            pltpu.VMEM((256, 1792), BF),
            pltpu.VMEM((2048, 512), BF),
            pltpu.VMEM((256, 2048), BF),
            pltpu.VMEM((512, 512), BF),
            pltpu.VMEM((2, BINS, 128), BF),
            pltpu.VMEM((GROUPS, 16, 128), BF),
            pltpu.VMEM((GROUPS, 16, 128), BF),
            pltpu.VMEM((GROUPS, 16, 128), BF),
            pltpu.VMEM((GROUPS, 16, 128), BF),
            [chunk_scratch(fours) for _, fours in CHUNKS],
            dma((6,)),
            dma, dma((count,)),
            dma, dma,
            dma((count, 6)), dma((count, 6)),
        ],
        compiler_params=pltpu.CompilerParams(
            collective_id=0, has_side_effects=True, vmem_limit_bytes=60 * 1024 * 1024
        ),
        name="moe_layer",
    )(tokens.T, expert_ids.T, gate_weights.T, gate_blocks, up_blocks, down_blocks)
    return combined.T


def solution(mesh):
    in_specs = (
        P("grp", "loc"),
        P("grp", None),
        P("grp", None),
        P(("grp", "loc"), None, None),
        P(("grp", "loc"), None, None),
        P(("grp", "loc"), None, None),
    )
    return jax.shard_map(
        shards, mesh=mesh, in_specs=in_specs, out_specs=P("grp", "loc"), check_vma=False
    )
```

time: 185 us -> 59.3 us (0.32)
  waiting for transfers between devices: 60.5 us -> 0 us
  Pallas kernels: 0 us -> 57.8 us
  blocking collectives: 51.2 us -> 0 us
  local copies, waits for them, and re-layouts: 38.6 us -> 1.36 us
  starting transfers between devices: 30.1 us -> 0 us
  other arithmetic: 2.02 us -> 0 us
    pallas_call x0 -> x1, Pallas kernels: none -> 57.8 us  [shards(): pl.pallas_call(kernel, out_shape=jax.ShapeDtypeStruct(tokens.shape[::-1],...]
    all_to_all x2 -> x0, blocking collectives: 51.2 us -> none  [the longest x1 26 us: shards(): lax.all_to_all(widened, 'loc', split_axis=2, concat_axis=2, tiled=True)]
    ppermute x5 -> x0, waiting for transfers between devices: 41.4 us -> none  [from_partner(): lax.ppermute(x, axis, [(i, i ^ 1 << distance) for i in range(lax.axis_siz...]
    all_to_all x2 -> x0, waiting for transfers between devices: 19.1 us -> none  [the longest x1 9.77 us: shards(): lax.all_to_all(lax.all_to_all(finished, 'grp', split_axis=0, concat_axis=...]
    ppermute x5 -> x0, starting transfers between devices: 18.2 us -> none  [from_partner(): lax.ppermute(x, axis, [(i, i ^ 1 << distance) for i in range(lax.axis_siz...]
    gather x13 -> x0, local copies, waits for them, and re-layouts: 14.6 us -> none  [the longest x5 8.91 us: bin_layout(): slot_index = jnp.take_along_axis(earlier, expert_ids, axis=1)]
    unnamed x18 -> x1, local copies, waits for them, and re-layouts: 13.7 us -> 1.36 us
    all_to_all x2 -> x0, starting transfers between devices: 11.9 us -> none  [the longest x1 8.42 us: shards(): lax.all_to_all(lax.all_to_all(finished, 'grp', split_axis=0, concat_axis=...]
  transfers between devices with their start and end apart: 7 -> 0, of which waited for: 7 -> 0; matrix products, arithmetic and copies ran while one was open for 0% -> 0% of each run, Pallas kernels for 0% -> 0%
where the time goes in v2:
time: 59.3 us; the launch traced here: 59.1 us
  Pallas kernels  57.8 us (97%)
  local copies, waits for them, and re-layouts  1.36 us (2%)
    pallas_call x1, Pallas kernels, shards(): pl.pallas_call(kernel, out_shape=jax.ShapeDtypeStruct(tokens.shape[::-1],...  57.8 us
    unnamed x1, local copies, waits for them, and re-layouts  1.36 us

profile of v2, /device:TPU:1, one launch (start us, length us, event | category | flops | bytes accessed | tf_op | source)
XLA Modules:
  0.0 59.1 jit_solution(6670245419499373640)
XLA Ops:
  0.0 57.8 %moe_layer.1 = bf16[112,128]{1,0:T(8,128)(2,1)} custom-call(bf16[112,128]{1,0:T(8,128)(2,1)} %bitcast.5, s32[8,128]{1,0:T(8,128)} %bitcast.6, f32[8,128]{1,0:T(8,128)} %bitcast.7, bf16[1,1792,256]{2,1,0:T(8,128)(2,1)} %wg_hbm.1, bf16[1,1792,256]{2,1,0:T(8,128)(2,1)} %wu_hbm.1, bf16[1,256,1792]{2,1,0:T(8,128)(2,1)} %wd_hbm.1), custom_call_target="tpu_custom_call" | custom-call | tf_op jit(solution)/shard_map/moe_layer/pallas_call | solution.py:364
  57.8 1.4 %copy.8 = bf16[128,112]{0,1:T(8,128)(2,1)} copy(bf16[128,112]{0,1:T(8,128)(2,1)} %bitcast.4) | data formatting | bytes 57344

commit v3 on v2

--- a/solution.py
+++ b/solution.py
@@ -115,12 +115,7 @@
 
     abuf[...] = jnp.zeros(abuf.shape, BF)
     b = iota((BINS, 128), 0)
-    n = b >> 4
-    half = (n + 1) >> 1
-    there = z - jnp.where((n & 1) == 1, half, -half)
-    there = jnp.where(there < 0, there + GROUPS, there)
-    there = jnp.where(there >= GROUPS, there - GROUPS, there)
-    e_b = there * 16 + ((b >> 3) & 1)
+    e_b = (b >> 4) * 16 + ((b >> 3) & 1)
     before = onehot(iota((128, 128), 0) < iota((128, 128), 1))
     for copy in loads[:3]:
         copy.wait()
@@ -149,17 +144,15 @@
 
     pl.semaphore_wait(barrier, GROUPS - 1 + CHIPS - 1 + 1)
 
-    for t, (first, fours) in reversed(list(enumerate(CHUNKS))):
-        low, high = max(1, 4 * first), 4 * (first + fours)
-
-        def send_a(i, carry, t=t, high=high):
-            s = high - 1 - i
-            g = lax.rem(z + GROUPS - offset(s), GROUPS)
-            send(abuf.at[s], r1.at[s], a_s, a_r.at[t], (g, l))
-            return carry
-
-        lax.fori_loop(0, high - low, send_a, 0)
-    r1[0] = abuf[0]
+    mine = lax.div(z, QUAD)
+    pltpu.make_async_copy(abuf.at[z], r1.at[z], a_r.at[mine]).start()
+
+    def send_a(i, carry):
+        g = lax.rem(z + GROUPS + offset(GROUPS - 1 - i), GROUPS)
+        send(abuf.at[g], r1.at[z], a_s, a_r.at[mine], (g, l))
+        return carry
+
+    lax.fori_loop(0, GROUPS - 1, send_a, 0)
 
     loads[3].wait()
     loads[4].wait()
@@ -179,20 +172,16 @@
         spread = onehot(((n & 31) < SUB) & (i == off + (n >> 5) * SUB + (n & 31)))
         dp[:, 128 * m : 128 * (m + 1)] = dot(wd[:, 128 * first : 128 * first + width], spread).astype(BF)
 
-    q = 2 * lax.rem(x, 2) + lax.div(y, 4)
-
-    def mate(k):
-        qq = lax.rem(q + k, 4)
-        there = LINE * (2 * lax.div(x, 2) + lax.div(qq, 2)) + 4 * lax.rem(qq, 2) + lax.rem(y, 4)
-        return (z, 2 * there + c)
-
-    A, PK, F, G, Y, C = range(6)
+    x_mate = (z, 2 * (chip + LINE * (1 - 2 * lax.rem(x, 2))) + c)
+    y_mate = (z, 2 * (LINE * x + lax.rem(y + 4, LINE)) + c)
+
+    PK, F, GX, GY, Y, C = range(6)
 
     def pack(t):
         first, fours = CHUNKS[t]
         pbuf, x2 = chunk_bufs[t][0:2]
         width = 8 * fours
-        wait_bytes(r1.at[pl.ds(0, 4 * fours - (1 if first == 0 else 0))], a_r.at[t])
+        wait_bytes(r1.at[pl.ds(4 * first, 4 * fours)], a_r.at[t])
         came = r1[4 * first : 4 * (first + fours)].astype(F32).reshape(fours, QUAD, 16, 128)
         left = [
             jnp.concatenate(
@@ -224,7 +213,7 @@
         send(x2.at[c], x2.at[c], chunk_s.at[t, F], chunk_r.at[t, F], partner)
 
     def gate_up(t):
-        x2, actf, gs, gr = chunk_bufs[t][1:5]
+        x2, actf, gx, gxr = chunk_bufs[t][1:5]
         width = 8 * CHUNKS[t][1]
         wait_bytes(x2.at[0], chunk_r.at[t, F])
         both = [x2[p].astype(F32).reshape(16, 2, width, 128) for p in range(2)]
@@ -233,17 +222,22 @@
         cols = [jnp.concatenate([w[r][m] for r in range(4)], axis=0).astype(BF) for m in range(16)]
         act = dot(jnp.concatenate(cols, axis=1), wp[...])
         actf[...] = act
-        gs[...] = act.astype(BF)
-        for k in (3, 1, 2):
-            send(gs, gr.at[k - 1], chunk_s.at[t, G], chunk_r.at[t, G], mate(k))
+        gx[...] = act.astype(BF)
+        send(gx, gxr, chunk_s.at[t, GX], chunk_r.at[t, GX], x_mate)
+
+    def gate_up_sum(t):
+        actf, gx, gxr, gy, gyr = chunk_bufs[t][2:7]
+        wait_bytes(gxr, chunk_r.at[t, GX])
+        act = actf[...] + gxr[...].astype(F32)
+        actf[...] = act
+        gy[...] = act.astype(BF)
+        send(gy, gyr, chunk_s.at[t, GY], chunk_r.at[t, GY], y_mate)
 
     def down(t):
-        actf, gs, gr, yb, yr = chunk_bufs[t][2:7]
+        actf, gx, gxr, gy, gyr, yb, yr = chunk_bufs[t][2:9]
         width = 8 * CHUNKS[t][1]
-        wait_bytes(gr, chunk_r.at[t, G])
-        act = actf[...]
-        for k in range(3):
-            act = act + gr[k].astype(F32)
+        wait_bytes(gyr, chunk_r.at[t, GY])
+        act = actf[...] + gyr[...].astype(F32)
         gate = act[:, 0:256]
         hidden = (gate * (1.0 / (1.0 + jnp.exp(-gate))) * act[:, 256:512]).astype(BF)
         part = dot(hidden, dp[...])
@@ -264,7 +258,7 @@
         send(yb.at[other], yr, chunk_s.at[t, Y], chunk_r.at[t, Y], partner)
 
     def spread_out(t):
-        yb, yr, cs, r3 = chunk_bufs[t][5:9]
+        yb, yr, cs, r3 = chunk_bufs[t][7:11]
         width = 8 * CHUNKS[t][1]
         wait_bytes(yr, chunk_r.at[t, Y])
         cs[...] = (yb[c].astype(F32) + yr[...].astype(F32)).astype(BF).reshape(CHIPS, width, 128)
@@ -281,7 +275,7 @@
 
     def home(t):
         first, fours = CHUNKS[t]
-        r3 = chunk_bufs[t][8]
+        r3 = chunk_bufs[t][10]
         width = 8 * fours
         wait_bytes(r3.at[pl.ds(0, CHIPS - 1)], chunk_r.at[t, C])
         parts = r3[...].astype(F32).reshape(8, 4, width, 128)
@@ -299,45 +293,50 @@
                     ],
                     axis=0,
                 ).astype(BF)
-        low, high = max(1, 4 * first), 4 * (first + fours)
-
-        def send_d(i, carry):
-            s = high - 1 - i
-            send(
-                dbuf.at[s], r4.at[s], d_s, d_r, (lax.rem(z + GROUPS + offset(s), GROUPS), l)
-            )
-            return carry
-
-        lax.fori_loop(0, high - low, send_d, 0)
-
-    count = len(CHUNKS)
-    for t in range(count):
+        for n in range(4 * fours):
+            group = 4 * first + n
+
+            @pl.when(z == group)
+            def _():
+                pltpu.make_async_copy(dbuf.at[group], r4.at[group], d_r).start()
+
+            @pl.when(z != group)
+            def _():
+                send(dbuf.at[group], r4.at[z], d_s, d_r, (group, l))
+
+    for t in range(len(CHUNKS)):
         pack(t)
-    for t in range(count):
-        forward(t)
-        if t >= 1:
-            gate_up(t - 1)
-    gate_up(count - 1)
-    for t in range(count):
-        down(t)
-        if t >= 1:
-            spread_out(t - 1)
-    spread_out(count - 1)
-    for t in reversed(range(count)):
-        home(t)
-    r4[0] = dbuf[0]
-    wait_bytes(r4.at[pl.ds(0, GROUPS - 1)], d_r)
+    forward(0)
+    gate_up(0)
+    forward(1)
+    forward(2)
+    gate_up_sum(0)
+    gate_up(1)
+    gate_up(2)
+    gate_up_sum(1)
+    gate_up_sum(2)
+    down(0)
+    spread_out(0)
+    down(1)
+    down(2)
+    spread_out(1)
+    spread_out(2)
+    home(0)
+    home(1)
+    home(2)
+    wait_bytes(r4, d_r)
     back = r4[...].reshape(BINS, 128)
     combined = dot(back, wt[0], ((0,), (0,))) + dot(back, wt[1], ((0,), (0,)))
     out_ref[...] = combined[0:112, :].astype(BF)
 
     wait_bytes(abuf.at[pl.ds(0, GROUPS - 1)], a_s)
     wait_bytes(dbuf.at[pl.ds(0, GROUPS - 1)], d_s)
-    for t in range(count):
-        x2, gr, yr, cs = (chunk_bufs[t][i] for i in (1, 4, 6, 7))
+    for t in range(len(CHUNKS)):
+        x2, gxr, gyr, yr, cs = (chunk_bufs[t][i] for i in (1, 4, 6, 8, 9))
         wait_bytes(x2.at[0, pl.ds(0, CHIPS - 1)], chunk_s.at[t, PK])
         wait_bytes(x2.at[0], chunk_s.at[t, F])
-        wait_bytes(gr, chunk_s.at[t, G])
+        wait_bytes(gxr, chunk_s.at[t, GX])
+        wait_bytes(gyr, chunk_s.at[t, GY])
         wait_bytes(yr, chunk_s.at[t, Y])
         wait_bytes(cs.at[pl.ds(0, CHIPS - 1)], chunk_s.at[t, C])
 
@@ -349,7 +348,9 @@
         pltpu.VMEM((2, CHIPS, width, 128), BF),
         pltpu.VMEM((4 * width, 512), F32),
         pltpu.VMEM((4 * width, 512), BF),
-        pltpu.VMEM((3, 4 * width, 512), BF),
+        pltpu.VMEM((4 * width, 512), BF),
+        pltpu.VMEM((4 * width, 512), BF),
+        pltpu.VMEM((4 * width, 512), BF),
         pltpu.VMEM((2, 16, 2, width, 128), BF),
         pltpu.VMEM((16, 2, width, 128), BF),
         pltpu.VMEM((CHIPS, width, 128), BF),

time: 59.3 us -> 55.4 us (0.934)
  Pallas kernels: 57.8 us -> 53.9 us
    pallas_call x1, Pallas kernels: 57.8 us -> 53.9 us  [shards(): pl.pallas_call(kernel, out_shape=jax.ShapeDtypeStruct(tokens.shape[::-1],...]
where the time goes in v3:
time: 55.4 us; the launch traced here: 55.2 us
  Pallas kernels  53.9 us (97%)
  local copies, waits for them, and re-layouts  1.36 us (2%)
    pallas_call x1, Pallas kernels, shards(): pl.pallas_call(kernel, out_shape=jax.ShapeDtypeStruct(tokens.shape[::-1],...  53.9 us
    unnamed x1, local copies, waits for them, and re-layouts  1.36 us

profile of v3, /device:TPU:1, one launch (start us, length us, event | category | flops | bytes accessed | tf_op | source)
XLA Modules:
  0.0 55.2 jit_solution(3219774711764808622)
XLA Ops:
  0.0 53.9 %moe_layer.1 = bf16[112,128]{1,0:T(8,128)(2,1)} custom-call(bf16[112,128]{1,0:T(8,128)(2,1)} %bitcast.5, s32[8,128]{1,0:T(8,128)} %bitcast.6, f32[8,128]{1,0:T(8,128)} %bitcast.7, bf16[1,1792,256]{2,1,0:T(8,128)(2,1)} %wg_hbm.1, bf16[1,1792,256]{2,1,0:T(8,128)(2,1)} %wu_hbm.1, bf16[1,256,1792]{2,1,0:T(8,128)(2,1)} %wd_hbm.1), custom_call_target="tpu_custom_call" | custom-call | tf_op jit(solution)/shard_map/moe_layer/pallas_call | solution.py:365
  53.9 1.4 %copy.8 = bf16[128,112]{0,1:T(8,128)(2,1)} copy(bf16[128,112]{0,1:T(8,128)(2,1)} %bitcast.4) | data formatting | bytes 57344

commit v4 on v3

--- a/solution.py
+++ b/solution.py
@@ -16,6 +16,7 @@
 QUAD = 4
 BINS = GROUPS * 16
 CHUNKS = ((0, 1), (1, 1), (2, 1))
+ONE_STEP = (0,)
 
 
 def iota(shape, dim):
@@ -173,6 +174,7 @@
         dp[:, 128 * m : 128 * (m + 1)] = dot(wd[:, 128 * first : 128 * first + width], spread).astype(BF)
 
     x_mate = (z, 2 * (chip + LINE * (1 - 2 * lax.rem(x, 2))) + c)
+    xy_mate = (z, 2 * (LINE * (x + 1 - 2 * lax.rem(x, 2)) + lax.rem(y + 4, LINE)) + c)
     y_mate = (z, 2 * (LINE * x + lax.rem(y + 4, LINE)) + c)
 
     PK, F, GX, GY, Y, C = range(6)
@@ -223,9 +225,16 @@
         act = dot(jnp.concatenate(cols, axis=1), wp[...])
         actf[...] = act
         gx[...] = act.astype(BF)
+        if t in ONE_STEP:
+            gr = chunk_bufs[t][11]
+            for k, there in enumerate((xy_mate, y_mate, x_mate)):
+                send(gx, gr.at[k], chunk_s.at[t, GX], chunk_r.at[t, GX], there)
+            return
         send(gx, gxr, chunk_s.at[t, GX], chunk_r.at[t, GX], x_mate)
 
     def gate_up_sum(t):
+        if t in ONE_STEP:
+            return
         actf, gx, gxr, gy, gyr = chunk_bufs[t][2:7]
         wait_bytes(gxr, chunk_r.at[t, GX])
         act = actf[...] + gxr[...].astype(F32)
@@ -236,8 +245,13 @@
     def down(t):
         actf, gx, gxr, gy, gyr, yb, yr = chunk_bufs[t][2:9]
         width = 8 * CHUNKS[t][1]
-        wait_bytes(gyr, chunk_r.at[t, GY])
-        act = actf[...] + gyr[...].astype(F32)
+        if t in ONE_STEP:
+            gr = chunk_bufs[t][11]
+            wait_bytes(gr, chunk_r.at[t, GX])
+            act = (actf[...] + gr[2].astype(F32)) + (gr[1].astype(F32) + gr[0].astype(F32))
+        else:
+            wait_bytes(gyr, chunk_r.at[t, GY])
+            act = actf[...] + gyr[...].astype(F32)
         gate = act[:, 0:256]
         hidden = (gate * (1.0 / (1.0 + jnp.exp(-gate))) * act[:, 256:512]).astype(BF)
         part = dot(hidden, dp[...])
@@ -254,14 +268,14 @@
             ]
         )
         for a in range(4):
-            yb[a % 2, :, a // 2] = w[a].astype(BF).reshape(16, width, 128)
+            yb[a % 2, :, a // 2] = w[a].reshape(16, width, 128)
         send(yb.at[other], yr, chunk_s.at[t, Y], chunk_r.at[t, Y], partner)
 
     def spread_out(t):
         yb, yr, cs, r3 = chunk_bufs[t][7:11]
         width = 8 * CHUNKS[t][1]
         wait_bytes(yr, chunk_r.at[t, Y])
-        cs[...] = (yb[c].astype(F32) + yr[...].astype(F32)).astype(BF).reshape(CHIPS, width, 128)
+        cs[...] = (yb[c] + yr[...]).astype(BF).reshape(CHIPS, width, 128)
 
         def send_c(i, carry):
             there = far_first(i)
@@ -324,21 +338,23 @@
     home(0)
     home(1)
     home(2)
+    wait_bytes(abuf.at[pl.ds(0, GROUPS - 1)], a_s)
+    for t in range(len(CHUNKS)):
+        x2, gxr, gyr, yr, cs = (chunk_bufs[t][i] for i in (1, 4, 6, 8, 9))
+        wait_bytes(x2.at[0, pl.ds(0, CHIPS - 1)], chunk_s.at[t, PK])
+        wait_bytes(x2.at[0], chunk_s.at[t, F])
+        if t in ONE_STEP:
+            wait_bytes(chunk_bufs[t][11], chunk_s.at[t, GX])
+        else:
+            wait_bytes(gxr, chunk_s.at[t, GX])
+            wait_bytes(gyr, chunk_s.at[t, GY])
+        wait_bytes(yr, chunk_s.at[t, Y])
+        wait_bytes(cs.at[pl.ds(0, CHIPS - 1)], chunk_s.at[t, C])
     wait_bytes(r4, d_r)
     back = r4[...].reshape(BINS, 128)
     combined = dot(back, wt[0], ((0,), (0,))) + dot(back, wt[1], ((0,), (0,)))
     out_ref[...] = combined[0:112, :].astype(BF)
-
-    wait_bytes(abuf.at[pl.ds(0, GROUPS - 1)], a_s)
     wait_bytes(dbuf.at[pl.ds(0, GROUPS - 1)], d_s)
-    for t in range(len(CHUNKS)):
-        x2, gxr, gyr, yr, cs = (chunk_bufs[t][i] for i in (1, 4, 6, 8, 9))
-        wait_bytes(x2.at[0, pl.ds(0, CHIPS - 1)], chunk_s.at[t, PK])
-        wait_bytes(x2.at[0], chunk_s.at[t, F])
-        wait_bytes(gxr, chunk_s.at[t, GX])
-        wait_bytes(gyr, chunk_s.at[t, GY])
-        wait_bytes(yr, chunk_s.at[t, Y])
-        wait_bytes(cs.at[pl.ds(0, CHIPS - 1)], chunk_s.at[t, C])
 
 
 def chunk_scratch(fours):
@@ -351,10 +367,11 @@
         pltpu.VMEM((4 * width, 512), BF),
         pltpu.VMEM((4 * width, 512), BF),
         pltpu.VMEM((4 * width, 512), BF),
-        pltpu.VMEM((2, 16, 2, width, 128), BF),
-        pltpu.VMEM((16, 2, width, 128), BF),
+        pltpu.VMEM((2, 16, 2, width, 128), F32),
+        pltpu.VMEM((16, 2, width, 128), F32),
         pltpu.VMEM((CHIPS, width, 128), BF),
         pltpu.VMEM((CHIPS, width, 128), BF),
+        pltpu.VMEM((3, 4 * width, 512), BF),
     ]
 
 

time: 55.4 us -> 54.7 us (0.987)
  Pallas kernels: 53.9 us -> 53.2 us
    pallas_call x1, Pallas kernels: 53.9 us -> 53.2 us  [shards(): pl.pallas_call(kernel, out_shape=jax.ShapeDtypeStruct(tokens.shape[::-1],...]
where the time goes in v4:
time: 54.7 us; the launch traced here: 54.5 us
  Pallas kernels  53.2 us (97%)
  local copies, waits for them, and re-layouts  1.36 us (2%)
    pallas_call x1, Pallas kernels, shards(): pl.pallas_call(kernel, out_shape=jax.ShapeDtypeStruct(tokens.shape[::-1],...  53.2 us
    unnamed x1, local copies, waits for them, and re-layouts  1.36 us

profile of v4, /device:TPU:1, one launch (start us, length us, event | category | flops | bytes accessed | tf_op | source)
XLA Modules:
  0.0 54.5 jit_solution(6876707143041873789)
XLA Ops:
  0.0 53.2 %moe_layer.1 = bf16[112,128]{1,0:T(8,128)(2,1)} custom-call(bf16[112,128]{1,0:T(8,128)(2,1)} %bitcast.5, s32[8,128]{1,0:T(8,128)} %bitcast.6, f32[8,128]{1,0:T(8,128)} %bitcast.7, bf16[1,1792,256]{2,1,0:T(8,128)(2,1)} %wg_hbm.1, bf16[1,1792,256]{2,1,0:T(8,128)(2,1)} %wu_hbm.1, bf16[1,256,1792]{2,1,0:T(8,128)(2,1)} %wd_hbm.1), custom_call_target="tpu_custom_call" | custom-call | tf_op jit(solution)/shard_map/moe_layer/pallas_call | solution.py:382
  53.2 1.4 %copy.8 = bf16[128,112]{0,1:T(8,128)(2,1)} copy(bf16[128,112]{0,1:T(8,128)(2,1)} %bitcast.4) | data formatting | bytes 57344

commit v5 on v4

--- a/solution.py
+++ b/solution.py
@@ -16,7 +16,7 @@
 QUAD = 4
 BINS = GROUPS * 16
 CHUNKS = ((0, 1), (1, 1), (2, 1))
-ONE_STEP = (0,)
+ONE_STEP = (0, 1)
 
 
 def iota(shape, dim):

time: 54.7 us -> 53.7 us (0.982)
  Pallas kernels: 53.2 us -> 52.2 us
    pallas_call x1, Pallas kernels: 53.2 us -> 52.2 us  [shards(): pl.pallas_call(kernel, out_shape=jax.ShapeDtypeStruct(tokens.shape[::-1],...]
where the time goes in v5:
time: 53.7 us; the launch traced here: 53.6 us
  Pallas kernels  52.2 us (97%)
  local copies, waits for them, and re-layouts  1.36 us (3%)
    pallas_call x1, Pallas kernels, shards(): pl.pallas_call(kernel, out_shape=jax.ShapeDtypeStruct(tokens.shape[::-1],...  52.2 us
    unnamed x1, local copies, waits for them, and re-layouts  1.36 us

profile of v5, /device:TPU:1, one launch (start us, length us, event | category | flops | bytes accessed | tf_op | source)
XLA Modules:
  0.0 53.6 jit_solution(3478166457291352678)
XLA Ops:
  0.0 52.2 %moe_layer.1 = bf16[112,128]{1,0:T(8,128)(2,1)} custom-call(bf16[112,128]{1,0:T(8,128)(2,1)} %bitcast.5, s32[8,128]{1,0:T(8,128)} %bitcast.6, f32[8,128]{1,0:T(8,128)} %bitcast.7, bf16[1,1792,256]{2,1,0:T(8,128)(2,1)} %wg_hbm.1, bf16[1,1792,256]{2,1,0:T(8,128)(2,1)} %wu_hbm.1, bf16[1,256,1792]{2,1,0:T(8,128)(2,1)} %wd_hbm.1), custom_call_target="tpu_custom_call" | custom-call | tf_op jit(solution)/shard_map/moe_layer/pallas_call | solution.py:382
  52.2 1.4 %copy.8 = bf16[128,112]{0,1:T(8,128)(2,1)} copy(bf16[128,112]{0,1:T(8,128)(2,1)} %bitcast.4) | data formatting | bytes 57344
